TPU v7x, 32 devices: a whole 2x2x4 slice. The times are simulated.
32 devices in a mesh: rows: 8 (over z, x), cols: 4 (over y, core).
Axes of the slice: x: 2, y: 2, z: 4, core: 2. Of those that a mesh axis runs over, the one named last changes fastest.
Arguments:
- points: float32 [24576, 1024], P('rows', 'cols'), may hold values from -80 to 80
- codes: int32 [128, 24576], P('cols', 'rows'), may hold values from 0 to 255, as said below
- rotation: float32 [1024, 1024], P('rows', 'cols'), may hold values from -0.16 to 1.16
Outputs:
- new_rotation: float32 [1024, 1024], P('rows', 'cols')
- centroids: float32 [128, 2048], P('cols')
Inputs may be any that keep to these rules, and one draw needn't show every extreme that they name: For every subspace, the first 256 vectors hold each of the 256 codes once.
All inputs are finite; a program needn't handle non-finite values.
Results may differ from a plain program's by a relative error of at most 0.00011.
Values sent between devices are 32-bit elements; how exact they have to be, the bound alone decides.
A program may use at most 128 MiB of HBM per device.

v0:
```python
import functools

import jax
import jax.numpy as jnp
from jax import lax
from jax.experimental import pallas as pl
from jax.experimental.pallas import tpu as pltpu
from jax.sharding import PartitionSpec as P

K = 256
NS_ITERS = 6
SUB = 8
LOW = 64
HIGH = K // LOW
GROUP = 4
F32 = jnp.float32
BF16 = jnp.bfloat16
MESH = pl.DeviceIdType.MESH
NT = (((1,), (1,)), ((), ()))
VMEM_BYTES = 56 * 1024 * 1024


def split(x):
    hi = x.astype(BF16)
    return hi, (x - hi.astype(F32)).astype(BF16)


def dot(left, right, dims):
    return lax.dot_general(left, right, dims, preferred_element_type=F32)


def dot3(left, right, dims):
    lh, ll = left
    rh, rl = right
    return dot(lh, rh, dims) + (dot(lh, rl, dims) + dot(ll, rh, dims))


def code_sums_kernel(codes_ref, rot_ref, sums_ref, counts_ref, left, right):
    n = codes_ref.shape[1]
    low_iota = lax.broadcasted_iota(jnp.int32, (LOW, n), 0)
    q_iota = lax.broadcasted_iota(jnp.int32, (8, n), 0)
    for g in range(codes_ref.shape[0] // GROUP):
        for i in range(GROUP):
            m = g * GROUP + i
            code = codes_ref[m : m + 1, :]
            q = code // LOW
            low = code - q * LOW
            right[i * LOW : (i + 1) * LOW, :] = jnp.where(low == low_iota, 1.0, 0.0).astype(BF16)
            value = rot_ref[m * SUB : (m + 1) * SUB, :]
            hi = value.astype(BF16).astype(F32)
            both = jnp.concatenate([hi, value - hi], axis=0)
            for h in range(HIGH):
                row = (i * HIGH + h) * 2 * SUB
                left[row : row + 2 * SUB, :] = jnp.where(q == h, both, 0.0).astype(BF16)
        for pair in range(GROUP // 2):
            row = 2 * SUB * HIGH * GROUP + pair * 16
            parts = []
            for i in range(2):
                m = g * GROUP + pair * 2 + i
                q = codes_ref[m : m + 1, :] // LOW
                parts.append(jnp.where(q == q_iota, 1.0, 0.0))
            left[row : row + 16, :] = jnp.concatenate(parts, axis=0).astype(BF16)
        out = dot(left[...], right[...], NT)
        for i in range(GROUP):
            m = g * GROUP + i
            lanes = slice(i * LOW, (i + 1) * LOW)
            pieces = []
            for h in range(HIGH):
                row = (i * HIGH + h) * 2 * SUB
                pieces.append(out[row : row + SUB, lanes] + out[row + SUB : row + 2 * SUB, lanes])
            sums_ref[m * SUB : (m + 1) * SUB, :] = jnp.concatenate(pieces, axis=1)
            row = 2 * SUB * HIGH * GROUP + i * 8
            counts_ref[m : m + 1, :] = jnp.concatenate(
                [out[row + h : row + h + 1, lanes] for h in range(HIGH)], axis=1
            )


def code_sums(codes, rot):
    subspaces, n = codes.shape
    block = 8
    rows = 2 * SUB * HIGH * GROUP + 8 * GROUP
    return pl.pallas_call(
        code_sums_kernel,
        grid=(subspaces // block,),
        in_specs=[
            pl.BlockSpec((block, n), lambda i: (i, 0)),
            pl.BlockSpec((block * SUB, n), lambda i: (i, 0)),
        ],
        out_specs=[
            pl.BlockSpec((block * SUB, K), lambda i: (i, 0)),
            pl.BlockSpec((block, K), lambda i: (i, 0)),
        ],
        out_shape=[
            jax.ShapeDtypeStruct((subspaces * SUB, K), F32),
            jax.ShapeDtypeStruct((subspaces, K), F32),
        ],
        scratch_shapes=[pltpu.VMEM((rows, n), BF16), pltpu.VMEM((GROUP * LOW, n), BF16)],
        compiler_params=pltpu.CompilerParams(vmem_limit_bytes=VMEM_BYTES),
        name="code_sums",
    )(codes, rot)


def cross_kernel(codes_ref, table_ref, points_ref, cross_ref, approx, phi, plo):
    subspaces, n = codes_ref.shape

    @pl.when(pl.program_id(0) == 0)
    def _():
        hi, lo = split(points_ref[...].T)
        phi[...] = hi
        plo[...] = lo

    for m in range(subspaces):
        rows = slice(m * SUB, (m + 1) * SUB)
        first = table_ref[rows, :128]
        second = table_ref[rows, 128:]
        for j in range(n // 128):
            lanes = slice(j * 128, (j + 1) * 128)
            code = jnp.broadcast_to(codes_ref[m : m + 1, lanes], (SUB, 128))
            inner = jnp.bitwise_and(code, 127)
            a = jnp.take_along_axis(first, inner, axis=1)
            b = jnp.take_along_axis(second, inner, axis=1)
            approx[rows, lanes] = jnp.where(code >= 128, b, a)
    cross_ref[...] = dot3((phi[...], plo[...]), split(approx[...]), NT)


def cross_terms(codes, table, points):
    subspaces, n = codes.shape
    d = points.shape[1]
    block = 32
    return pl.pallas_call(
        cross_kernel,
        grid=(subspaces // block,),
        in_specs=[
            pl.BlockSpec((block, n), lambda i: (i, 0)),
            pl.BlockSpec((block * SUB, K), lambda i: (i, 0)),
            pl.BlockSpec((n, d), lambda i: (0, 0)),
        ],
        out_specs=pl.BlockSpec((d, block * SUB), lambda i: (0, i)),
        out_shape=jax.ShapeDtypeStruct((d, subspaces * SUB), F32),
        scratch_shapes=[
            pltpu.VMEM((block * SUB, n), F32),
            pltpu.VMEM((d, n), BF16),
            pltpu.VMEM((d, n), BF16),
        ],
        compiler_params=pltpu.CompilerParams(vmem_limit_bytes=VMEM_BYTES),
        name="cross_terms",
    )(codes, table, points)


def bits(size):
    return size.bit_length() - 1


def partner_of(axis, bit):
    me = lax.axis_index(axis)
    mine = (me // (1 << bit)) % 2
    return mine, {axis: me + (1 - 2 * mine) * (1 << bit)}


def enter(steps):
    barrier = pltpu.get_barrier_semaphore()
    for axis, bit in steps:
        pl.semaphore_signal(barrier, inc=1, device_id=partner_of(axis, bit)[1], device_id_type=MESH)
    pl.semaphore_wait(barrier, len(steps))


def table_kernel(steps, copies, part_ref, table_ref, acc, landing, send, recv):
    chunks, height, _ = part_ref.shape
    sums = table_ref.shape[1]
    enter(steps)
    lo = 0
    half = chunks // 2
    offset = 0
    for t, (axis, bit) in enumerate(steps):
        mine, partner = partner_of(axis, bit)
        source = part_ref if t == 0 else acc
        keep = lo + mine * half
        away = lo + (1 - mine) * half
        copy = pltpu.make_async_remote_copy(
            src_ref=source.at[pl.ds(away, half)],
            dst_ref=landing.at[pl.ds(offset, half)],
            send_sem=send.at[t],
            recv_sem=recv.at[t],
            device_id=partner,
            device_id_type=MESH,
        )
        copy.start()
        copy.wait()
        acc[pl.ds(keep, half)] = source[pl.ds(keep, half)] + landing[pl.ds(offset, half)]
        lo = keep
        offset += half
        half = half // 2
    mine = acc[lo]
    pieces = []
    for i in range(sums // SUB):
        count = mine[sums + i : sums + i + 1, :] * (1.0 / copies)
        pieces.append(mine[i * SUB : (i + 1) * SUB, :] / count)
    table_ref[lo] = jnp.concatenate(pieces, axis=0)
    size = 1
    for t, (axis, bit) in enumerate(reversed(steps)):
        mine, partner = partner_of(axis, bit)
        copy = pltpu.make_async_remote_copy(
            src_ref=table_ref.at[pl.ds(lo, size)],
            dst_ref=table_ref.at[pl.ds(lo, size)],
            send_sem=send.at[len(steps) + t],
            recv_sem=recv.at[len(steps) + t],
            device_id=partner,
            device_id_type=MESH,
        )
        copy.start()
        copy.wait()
        lo = lo - mine * size
        size = size * 2


def centroid_table(sums, counts, nr, nc):
    chunks = nr * nc
    own = counts.shape[0] // chunks
    counts = counts.reshape(chunks, own, K)
    pad = -own % 8
    part = jnp.concatenate(
        [sums.reshape(chunks, own * SUB, K), jnp.pad(counts, ((0, 0), (0, pad), (0, 0)))], axis=1
    )
    steps = [("cols", b) for b in range(bits(nc))] + [("rows", b) for b in range(bits(nr))]
    vmem = pl.BlockSpec(memory_space=pltpu.VMEM)
    table = pl.pallas_call(
        functools.partial(table_kernel, steps, nc),
        in_specs=[vmem],
        out_specs=vmem,
        out_shape=jax.ShapeDtypeStruct((chunks, own * SUB, K), F32),
        scratch_shapes=[
            pltpu.VMEM(part.shape, F32),
            pltpu.VMEM(part.shape, F32),
            pltpu.SemaphoreType.DMA((2 * len(steps),)),
            pltpu.SemaphoreType.DMA((2 * len(steps),)),
        ],
        compiler_params=pltpu.CompilerParams(
            collective_id=0, has_side_effects=True, vmem_limit_bytes=VMEM_BYTES
        ),
        name="centroid_table",
    )(part)
    return table.reshape(sums.shape)


def remote(src, dst, send, recv, index, partner):
    return pltpu.make_async_remote_copy(
        src_ref=src,
        dst_ref=dst,
        send_sem=send.at[index],
        recv_sem=recv.at[index],
        device_id=partner,
        device_id_type=MESH,
    )


def gather_cross_kernel(parts, steps, part_ref, full_ref, acc, landing, send, recv):
    chunks = part_ref.shape[0]
    c = lax.axis_index("cols")
    enter(steps)
    sem = 0
    lows = [0] * len(parts)
    half = chunks // 2
    offset = 0
    for t in range(bits(chunks)):
        copies = []
        for i, (lanes, halving, _) in enumerate(parts):
            mine, partner = partner_of(*halving[t])
            source = part_ref if t == 0 else acc
            away = lows[i] + (1 - mine) * half
            copies.append(
                remote(
                    source.at[pl.ds(away, half), :, lanes],
                    landing.at[pl.ds(offset, half), :, lanes],
                    send,
                    recv,
                    sem,
                    partner,
                )
            )
            sem += 1
            copies[-1].start()
        for i, (lanes, halving, _) in enumerate(parts):
            mine, partner = partner_of(*halving[t])
            source = part_ref if t == 0 else acc
            keep = lows[i] + mine * half
            copies[i].wait()
            total = source[pl.ds(keep, half), :, lanes] + landing[pl.ds(offset, half), :, lanes]
            if half == 1:
                full_ref[c, pl.ds(keep, half), :, lanes] = total
            else:
                acc[pl.ds(keep, half), :, lanes] = total
            lows[i] = keep
        offset += half
        half = half // 2
    sizes = [1] * len(parts)
    held = [[c] for _ in parts]
    for t in range(len(steps)):
        copies = []
        for i, (lanes, _, doubling) in enumerate(parts):
            axis, bit = doubling[t]
            mine, partner = partner_of(axis, bit)
            for block in held[i]:
                ref = full_ref.at[block, pl.ds(lows[i], sizes[i]), :, lanes]
                copies.append(remote(ref, ref, send, recv, sem, partner))
                copies[-1].start()
                sem += 1
            if axis == "rows":
                lows[i] = lows[i] - mine * sizes[i]
                sizes[i] = sizes[i] * 2
            else:
                held[i] = held[i] + [block + (1 - 2 * mine) * (1 << bit) for block in held[i]]
        for copy in copies:
            copy.wait()


def gather_cross(part, nr, nc):
    d, width = part.shape
    part = part.reshape(nr, d // nr, width)
    rows = [("rows", b) for b in range(bits(nr))]
    cols = [("cols", b) for b in reversed(range(bits(nc)))]
    late = rows[1:] + rows[:1]
    unit = width // 8
    back, back_late = rows[::-1], late[::-1]
    parts = [
        (slice(0, 3 * unit), rows, back + cols),
        (slice(3 * unit, 6 * unit), rows, back[:-1] + cols[:1] + back[-1:] + cols[1:]),
        (slice(6 * unit, width), late, back_late[:1] + cols[:1] + back_late[1:] + cols[1:]),
    ]
    sems = 3 * (len(rows) + len(rows) * (nc // 2) + nc)
    vmem = pl.BlockSpec(memory_space=pltpu.VMEM)
    full = pl.pallas_call(
        functools.partial(gather_cross_kernel, parts, rows + cols),
        in_specs=[vmem],
        out_specs=vmem,
        out_shape=jax.ShapeDtypeStruct((nc,) + part.shape, F32),
        scratch_shapes=[
            pltpu.VMEM(part.shape, F32),
            pltpu.VMEM(part.shape, F32),
            pltpu.SemaphoreType.DMA((sems,)),
            pltpu.SemaphoreType.DMA((sems,)),
        ],
        compiler_params=pltpu.CompilerParams(
            collective_id=1, has_side_effects=True, vmem_limit_bytes=VMEM_BYTES
        ),
        name="gather_cross",
    )(part)
    return full.reshape(nc * d, width)


def reversed_bits(index, count):
    out = 0
    for b in range(count):
        out = out + ((index // (1 << b)) % 2) * (1 << (count - 1 - b))
    return out


def gather_inputs_kernel(row_steps, col_steps, rot_ref, codes_ref, rows_ref, all_codes, send, recv, own_sem):
    nr, piece, _ = rows_ref.shape
    nc = all_codes.shape[0]
    width = rot_ref.shape[1]
    r, c = lax.axis_index("rows"), lax.axis_index("cols")
    place = reversed_bits(r, len(row_steps))
    source = (c * nr + place) // nc
    is_own = source == r
    barrier = pltpu.get_barrier_semaphore()
    for j in range(nc):

        @pl.when(jnp.logical_not(is_own & (c == j)))
        def _():
            pl.semaphore_signal(barrier, inc=1, device_id=(source, j), device_id_type=MESH)

    for axis, bit in row_steps + col_steps:
        pl.semaphore_signal(barrier, inc=1, device_id=partner_of(axis, bit)[1], device_id_type=MESH)
    count = nc + len(row_steps) + len(col_steps)
    pl.semaphore_wait(barrier, jnp.where(is_own, count - 1, count))

    lanes = pl.ds(pl.multiple_of(c * width, width), width)
    partners = [partner_of(axis, bit) for axis, bit in col_steps]
    sem = 2 * nc
    first = remote(codes_ref, all_codes.at[c], send, recv, sem, partners[0][1])
    first.start()
    sem += 1
    sends = []
    for i in range(nc):
        g = r * nc + i
        to_c, to_place = g // nr, g % nr
        to_r = reversed_bits(to_place, len(row_steps))
        src = rot_ref.at[pl.ds(i * piece, piece), :]
        dst = rows_ref.at[to_place, :, lanes]
        stays = (to_c == c) & (to_r == r)
        copy = pltpu.make_async_remote_copy(
            src_ref=src,
            dst_ref=dst,
            send_sem=send.at[i],
            recv_sem=recv.at[c],
            device_id=(to_r, to_c),
            device_id_type=MESH,
        )
        sends.append((stays, copy))

        @pl.when(stays)
        def _():
            local = pltpu.make_async_copy(src, dst, own_sem)
            local.start()
            local.wait()

        @pl.when(jnp.logical_not(stays))
        def _():
            copy.start()

    all_codes[c] = codes_ref[...]
    for j in range(nc):

        @pl.when(jnp.logical_not(is_own & (c == j)))
        def _():
            ref = rows_ref.at[place, :, pl.ds(j * width, width)]
            remote(ref, ref, send, recv, j, partners[0][1]).wait_recv()

    lo, size = place, 1
    held = [c]
    mine, partner = partners[0]
    after = [c + (1 - 2 * mine) * (1 << col_steps[0][1])]
    for t, (axis, bit) in enumerate(reversed(row_steps)):
        mine, partner = partner_of(axis, bit)
        ref = rows_ref.at[pl.ds(lo, size)]
        copy = remote(ref, ref, send, recv, sem, partner)
        sem += 1
        copy.start()
        copy.wait()
        lo = lo - mine * size
        size = size * 2
    first.wait()
    held = held + after
    for (mine, partner), (axis, bit) in list(zip(partners, col_steps))[1:]:
        copies = []
        for block in held:
            ref = all_codes.at[block]
            copies.append(remote(ref, ref, send, recv, sem, partner))
            sem += 1
            copies[-1].start()
        for copy in copies:
            copy.wait()
        held = held + [block + (1 - 2 * mine) * (1 << bit) for block in held]
    for stays, copy in sends:

        @pl.when(jnp.logical_not(stays))
        def _():
            copy.wait_send()


def gather_inputs(rotation, codes, nr, nc):
    height, width = rotation.shape
    row_steps = [("rows", b) for b in range(bits(nr))]
    col_steps = [("cols", b) for b in reversed(range(bits(nc)))]
    vmem = pl.BlockSpec(memory_space=pltpu.VMEM)
    sems = 3 * nc + len(row_steps)
    rows, all_codes = pl.pallas_call(
        functools.partial(gather_inputs_kernel, row_steps, col_steps),
        in_specs=[vmem, vmem],
        out_specs=[vmem, vmem],
        out_shape=[
            jax.ShapeDtypeStruct((nr, height // nc, nc * width), F32),
            jax.ShapeDtypeStruct((nc,) + codes.shape, codes.dtype),
        ],
        scratch_shapes=[
            pltpu.SemaphoreType.DMA((sems,)),
            pltpu.SemaphoreType.DMA((sems,)),
            pltpu.SemaphoreType.DMA,
        ],
        compiler_params=pltpu.CompilerParams(
            collective_id=2, has_side_effects=True, vmem_limit_bytes=VMEM_BYTES
        ),
        name="gather_inputs",
    )(rotation, codes)
    return rows.reshape(nr * height // nc, nc * width), all_codes.reshape(-1, codes.shape[1])


def iterate_kernel(cross_ref, out_ref, hi, lo, own, landing, total, send, recv):
    size = cross_ref.shape[0]
    half = size // 2
    tile = half // 2
    mine, partner = partner_of("cols", 0)
    enter([("cols", 0)])
    band = size // 8

    total[...] = jnp.zeros_like(total)

    @pl.loop(0, 8)
    def _(i):
        x = cross_ref[pl.ds(pl.multiple_of(i * band, band), band), :]
        total[...] += jnp.sum((x * x).reshape(band // 8, 8, size), axis=0)

    scale = 1.7 / jnp.sqrt(jnp.sum(total[...], keepdims=True) + 1e-06)

    @pl.loop(0, 8)
    def _(i):
        rows = pl.ds(pl.multiple_of(i * band, band), band)
        h, l = split(cross_ref[rows, :] * scale)
        hi[rows, :] = h
        lo[rows, :] = l

    nn = (((1,), (0,)), ((), ()))

    @pl.loop(0, NS_ITERS - 1)
    def _(step):
        slot = step % 2

        def sent(t):
            rows = pl.ds(t * tile, tile)
            return pltpu.make_async_remote_copy(
                src_ref=own.at[rows, :],
                dst_ref=landing.at[slot, rows, :],
                send_sem=send.at[slot, t],
                recv_sem=recv.at[slot, t],
                device_id=partner,
                device_id_type=MESH,
            )

        for t in range(2):
            rows = pl.ds(pl.multiple_of(mine * half + t * tile, tile), tile)
            xh, xl = hi[rows, :], lo[rows, :]
            gram = dot3((xh, xl), (hi[...], lo[...]), NT)
            x = xh.astype(F32) + xl.astype(F32)
            own[t * tile : (t + 1) * tile, :] = 1.5 * x - 0.5 * dot3(
                split(gram), (hi[...], lo[...]), nn
            )
            sent(t).start()
        for t in range(2):
            rows = pl.ds(pl.multiple_of(mine * half + t * tile, tile), tile)
            h, l = split(own[t * tile : (t + 1) * tile, :])
            hi[rows, :] = h
            lo[rows, :] = l
        for t in range(2):
            rows = pl.ds(pl.multiple_of((1 - mine) * half + t * tile, tile), tile)
            sent(t).wait()
            h, l = split(landing[slot, t * tile : (t + 1) * tile, :])
            hi[rows, :] = h
            lo[rows, :] = l

    height, width = out_ref.shape
    r, c = lax.axis_index("rows"), lax.axis_index("cols")
    rows = pl.ds(pl.multiple_of(r * height, height), height)
    columns = pl.ds(pl.multiple_of(c * width, width), width)
    gram = dot3((hi[rows, :], lo[rows, :]), (hi[...], lo[...]), NT)
    x = hi[rows, columns].astype(F32) + lo[rows, columns].astype(F32)
    x = 1.5 * x - 0.5 * dot3(split(gram), (hi[:, columns], lo[:, columns]), nn)
    out_ref[...] = x * size**0.5


def new_rotation(cross, shape):
    size = cross.shape[0]
    vmem = pl.BlockSpec(memory_space=pltpu.VMEM)
    return pl.pallas_call(
        iterate_kernel,
        in_specs=[vmem],
        out_specs=vmem,
        out_shape=jax.ShapeDtypeStruct(shape, F32),
        scratch_shapes=[
            pltpu.VMEM((size, size), BF16),
            pltpu.VMEM((size, size), BF16),
            pltpu.VMEM((size // 2, size), F32),
            pltpu.VMEM((2, size // 2, size), F32),
            pltpu.VMEM((8, size), F32),
            pltpu.SemaphoreType.DMA((2, 2)),
            pltpu.SemaphoreType.DMA((2, 2)),
        ],
        compiler_params=pltpu.CompilerParams(
            collective_id=3, has_side_effects=True, vmem_limit_bytes=VMEM_BYTES
        ),
        name="new_rotation",
    )(cross)


def matmul_high(left, right, dims):
    return lax.dot_general(
        left, right, dims, precision=lax.Precision.HIGH, preferred_element_type=F32
    )


def shards(nr, nc, points, codes, rotation):
    own_rows, all_codes = gather_inputs(rotation, codes, nr, nc)
    rotated = matmul_high(own_rows, points, (((0,), (1,)), ((), ())))
    sums, counts = code_sums(all_codes, rotated)
    table = centroid_table(sums, counts, nr, nc)
    c = lax.axis_index("cols")
    local = codes.shape[0]
    own = lax.dynamic_slice_in_dim(table, c * local * SUB, local * SUB, 0)
    centroids = own.reshape(local, SUB, K).transpose(0, 2, 1).reshape(local, K * SUB)
    cross = gather_cross(cross_terms(all_codes, table, points), nr, nc)
    return (new_rotation(cross, rotation.shape), centroids)


def solution(mesh):
    nr, nc = mesh.shape["rows"], mesh.shape["cols"]
    in_specs = (P("rows", "cols"), P("cols", "rows"), P("rows", "cols"))
    out_specs = (P("rows", "cols"), P("cols", None))
    return jax.shard_map(
        functools.partial(shards, nr, nc),
        mesh=mesh,
        in_specs=in_specs,
        out_specs=out_specs,
        check_vma=False,
    )
```

profile of v0, /device:TPU:0, one launch (start us, length us, event | category | flops | bytes accessed | tf_op | source)
XLA Modules:
  0.0 271.9 jit_solution(2153212626592261463)
XLA Ops:
  0.6 41.8 %gather_inputs.1 = (f32[8,32,1024]{2,1,0:T(8,128)}, s32[4,32,3072]{2,1,0:T(8,128)}) custom-call(f32[128,256]{1,0:T(8,128)} %rot_ref.1, s32[32,3072]{1,0:T(8,128)} %codes_ref.1), custom_call_target="tpu_custom_call" | custom-call | tf_op jit(solution)/shard_map/gather_inputs/pallas_call | solution.py:457
  42.5 14.5 %fusion.rot_ref = f32[1024,3072]{1,0:T(8,128)} fusion(f32[256,1024]{1,0:T(8,128)} %bitcast.20, f32[3072,256]{1,0:T(8,128)} %points_ref.1), kind=kOutput, calls=%fused_computation.3 | convolution fusion | flops 4831838208 | bytes 16777216 | tf_op jit(solution)/shard_map/dot_general | solution.py:575
  57.0 24.6 %code_sums.1 = (f32[1024,256]{1,0:T(8,128)}, f32[128,256]{1,0:T(8,128)}) custom-call(s32[128,3072]{1,0:T(8,128)} %bitcast.14, f32[1024,3072]{1,0:T(8,128)} %fusion.rot_ref), custom_call_target="tpu_custom_call" | custom-call | tf_op jit(solution)/shard_map/code_sums/pallas_call | solution.py:82
  81.6 0.9 reshape.34
  82.5 2.4 select_maximum_fusion.part_ref
  85.0 46.3 %centroid_table.1 = f32[32,32,256]{2,1,0:T(8,128)} custom-call(f32[32,40,256]{2,1,0:T(8,128)} %select_maximum_fusion.part_ref), custom_call_target="tpu_custom_call" | custom-call | tf_op jit(solution)/shard_map/centroid_table/pallas_call | solution.py:226
  131.3 1.0 dynamic-slice_bitcast_fusion
  132.2 0.4 copy.5
  132.7 1.0 copy.6
  133.7 23.5 %cross_terms.1 = f32[256,1024]{1,0:T(8,128)} custom-call(s32[128,3072]{1,0:T(8,128)} %bitcast.15, f32[1024,256]{1,0:T(8,128)} %bitcast.17, f32[3072,256]{1,0:T(8,128)} %points_ref.1), custom_call_target="tpu_custom_call" | custom-call | tf_op jit(solution)/shard_map/cross_terms/pallas_call | solution.py:130
  157.2 58.6 %gather_cross.1 = f32[4,8,32,1024]{3,2,1,0:T(8,128)} custom-call(f32[8,32,1024]{2,1,0:T(8,128)} %bitcast.19), custom_call_target="tpu_custom_call" | custom-call | tf_op jit(solution)/shard_map/gather_cross/pallas_call | solution.py:331
  215.8 54.5 %new_rotation.1 = f32[128,256]{1,0:T(8,128)} custom-call(f32[1024,1024]{1,0:T(8,128)} %bitcast.13), custom_call_target="tpu_custom_call" | custom-call | tf_op jit(solution)/shard_map/new_rotation/pallas_call | solution.py:553
  270.4 1.6 copy.8
where the time goes:
time: 272 us
  Pallas kernels  249 us (92%)
  matrix products  14.5 us (5%)
  local copies, waits for them, and re-layouts  4.94 us (2%)
    pallas_call x1, Pallas kernels, gather_cross(): pl.pallas_call(functools.partial(gather_cross_kernel, parts, rows + cols)...  58.6 us
    pallas_call x1, Pallas kernels, new_rotation(): pl.pallas_call(iterate_kernel, in_specs=[vmem], out_specs=vmem, out_shape...  54.5 us
    pallas_call x1, Pallas kernels, centroid_table(): pl.pallas_call(functools.partial(table_kernel, steps, nc), in_specs=[vmem...  46.3 us
    pallas_call x1, Pallas kernels, gather_inputs(): pl.pallas_call(functools.partial(gather_inputs_kernel, row_steps, col_ste...  41.8 us
    pallas_call x1, Pallas kernels, code_sums(): pl.pallas_call(code_sums_kernel, grid=(subspaces // block,), in_specs=[pl...  24.6 us
    pallas_call x1, Pallas kernels, cross_terms(): pl.pallas_call(cross_kernel, grid=(subspaces // block,), in_specs=[pl.Blo...  23.5 us
    dot_general x1, matrix products, matmul_high(): lax.dot_general(left, right, dims, precision=lax.Precision.HIGH, preferre...  14.5 us

commit v1 on v0

--- a/solution.py
+++ b/solution.py
@@ -35,69 +35,94 @@
     return dot(lh, rh, dims) + (dot(lh, rl, dims) + dot(ll, rh, dims))
 
 
-def code_sums_kernel(codes_ref, rot_ref, sums_ref, counts_ref, left, right):
+def code_sums_kernel(codes_ref, rows_ref, points_ref, part_ref, left, right, phi, plo, rotated):
+    step = pl.program_id(0)
     n = codes_ref.shape[1]
-    low_iota = lax.broadcasted_iota(jnp.int32, (LOW, n), 0)
-    q_iota = lax.broadcasted_iota(jnp.int32, (8, n), 0)
-    for g in range(codes_ref.shape[0] // GROUP):
+    block = codes_ref.shape[0]
+    own = block // part_ref.shape[0]
+    panel = rows_ref.shape[1]
+    turns = panel // (block * SUB)
+
+    @pl.when(step == 0)
+    def _():
+        hi, lo = split(points_ref[...])
+        phi[...] = hi
+        plo[...] = lo
+
+    @pl.when(step % turns == 0)
+    def _():
+        rotated[...] = dot3(split(rows_ref[...].T), (phi[...], plo[...]), NT)
+
+    base = (step % turns) * (block * SUB)
+    iota = lax.broadcasted_iota(jnp.int32, (16, n), 0)
+    iota_16 = iota.astype(F32).astype(BF16)
+    iota_8 = (iota % 8).astype(F32).astype(BF16)
+    one, zero = jnp.ones((16, n), BF16), jnp.zeros((16, n), BF16)
+    part_ref[...] = jnp.zeros_like(part_ref)
+    for g in range(block // GROUP):
         for i in range(GROUP):
             m = g * GROUP + i
-            code = codes_ref[m : m + 1, :]
-            q = code // LOW
-            low = code - q * LOW
-            right[i * LOW : (i + 1) * LOW, :] = jnp.where(low == low_iota, 1.0, 0.0).astype(BF16)
-            value = rot_ref[m * SUB : (m + 1) * SUB, :]
+            code = jnp.broadcast_to(codes_ref[m : m + 1, :], (16, n))
+            q_int = code >> bits(LOW)
+            low = jnp.bitwise_and(code, LOW - 1).astype(F32).astype(BF16)
+            q = q_int.astype(F32).astype(BF16)
+            for k in range(LOW // 16):
+                row = i * LOW + k * 16
+                right[row : row + 16, :] = jnp.where(low - 16 * k == iota_16, one, zero)
+            value = rotated[pl.ds(pl.multiple_of(base + m * SUB, SUB), SUB), :]
             hi = value.astype(BF16).astype(F32)
-            both = jnp.concatenate([hi, value - hi], axis=0)
+            both = jnp.concatenate([hi, value - hi], axis=0).astype(BF16)
             for h in range(HIGH):
                 row = (i * HIGH + h) * 2 * SUB
-                left[row : row + 2 * SUB, :] = jnp.where(q == h, both, 0.0).astype(BF16)
-        for pair in range(GROUP // 2):
-            row = 2 * SUB * HIGH * GROUP + pair * 16
-            parts = []
-            for i in range(2):
-                m = g * GROUP + pair * 2 + i
-                q = codes_ref[m : m + 1, :] // LOW
-                parts.append(jnp.where(q == q_iota, 1.0, 0.0))
-            left[row : row + 16, :] = jnp.concatenate(parts, axis=0).astype(BF16)
+                left[row : row + 2 * SUB, :] = jnp.where(q == h, both, zero)
+            row = 2 * SUB * HIGH * GROUP + i * 16
+            left[row : row + 16, :] = jnp.where(q == iota_8, one, zero)
         out = dot(left[...], right[...], NT)
         for i in range(GROUP):
             m = g * GROUP + i
+            chunk, place = m // own, m % own
             lanes = slice(i * LOW, (i + 1) * LOW)
             pieces = []
             for h in range(HIGH):
                 row = (i * HIGH + h) * 2 * SUB
                 pieces.append(out[row : row + SUB, lanes] + out[row + SUB : row + 2 * SUB, lanes])
-            sums_ref[m * SUB : (m + 1) * SUB, :] = jnp.concatenate(pieces, axis=1)
-            row = 2 * SUB * HIGH * GROUP + i * 8
-            counts_ref[m : m + 1, :] = jnp.concatenate(
+            part_ref[chunk, place * SUB : (place + 1) * SUB, :] = jnp.concatenate(pieces, axis=1)
+            row = 2 * SUB * HIGH * GROUP + i * 16
+            place = own * SUB + place
+            part_ref[chunk, place : place + 1, :] = jnp.concatenate(
                 [out[row + h : row + h + 1, lanes] for h in range(HIGH)], axis=1
             )
 
 
-def code_sums(codes, rot):
+def code_sums(codes, own_rows, points, chunks):
     subspaces, n = codes.shape
+    d = points.shape[1]
     block = 8
-    rows = 2 * SUB * HIGH * GROUP + 8 * GROUP
+    own = subspaces // chunks
+    panel = 256
+    turns = panel // (block * SUB)
+    height = own * SUB + own + -own % 8
+    rows = 2 * SUB * HIGH * GROUP + 16 * GROUP
     return pl.pallas_call(
         code_sums_kernel,
         grid=(subspaces // block,),
         in_specs=[
             pl.BlockSpec((block, n), lambda i: (i, 0)),
-            pl.BlockSpec((block * SUB, n), lambda i: (i, 0)),
-        ],
-        out_specs=[
-            pl.BlockSpec((block * SUB, K), lambda i: (i, 0)),
-            pl.BlockSpec((block, K), lambda i: (i, 0)),
-        ],
-        out_shape=[
-            jax.ShapeDtypeStruct((subspaces * SUB, K), F32),
-            jax.ShapeDtypeStruct((subspaces, K), F32),
-        ],
-        scratch_shapes=[pltpu.VMEM((rows, n), BF16), pltpu.VMEM((GROUP * LOW, n), BF16)],
+            pl.BlockSpec((d, panel), lambda i: (0, i // turns)),
+            pl.BlockSpec((n, d), lambda i: (0, 0)),
+        ],
+        out_specs=pl.BlockSpec((block // own, height, K), lambda i: (i, 0, 0)),
+        out_shape=jax.ShapeDtypeStruct((chunks, height, K), F32),
+        scratch_shapes=[
+            pltpu.VMEM((rows, n), BF16),
+            pltpu.VMEM((GROUP * LOW, n), BF16),
+            pltpu.VMEM((n, d), BF16),
+            pltpu.VMEM((n, d), BF16),
+            pltpu.VMEM((panel, n), F32),
+        ],
         compiler_params=pltpu.CompilerParams(vmem_limit_bytes=VMEM_BYTES),
         name="code_sums",
-    )(codes, rot)
+    )(codes, own_rows, points)
 
 
 def cross_kernel(codes_ref, table_ref, points_ref, cross_ref, approx, phi, plo):
@@ -164,84 +189,6 @@
     pl.semaphore_wait(barrier, len(steps))
 
 
-def table_kernel(steps, copies, part_ref, table_ref, acc, landing, send, recv):
-    chunks, height, _ = part_ref.shape
-    sums = table_ref.shape[1]
-    enter(steps)
-    lo = 0
-    half = chunks // 2
-    offset = 0
-    for t, (axis, bit) in enumerate(steps):
-        mine, partner = partner_of(axis, bit)
-        source = part_ref if t == 0 else acc
-        keep = lo + mine * half
-        away = lo + (1 - mine) * half
-        copy = pltpu.make_async_remote_copy(
-            src_ref=source.at[pl.ds(away, half)],
-            dst_ref=landing.at[pl.ds(offset, half)],
-            send_sem=send.at[t],
-            recv_sem=recv.at[t],
-            device_id=partner,
-            device_id_type=MESH,
-        )
-        copy.start()
-        copy.wait()
-        acc[pl.ds(keep, half)] = source[pl.ds(keep, half)] + landing[pl.ds(offset, half)]
-        lo = keep
-        offset += half
-        half = half // 2
-    mine = acc[lo]
-    pieces = []
-    for i in range(sums // SUB):
-        count = mine[sums + i : sums + i + 1, :] * (1.0 / copies)
-        pieces.append(mine[i * SUB : (i + 1) * SUB, :] / count)
-    table_ref[lo] = jnp.concatenate(pieces, axis=0)
-    size = 1
-    for t, (axis, bit) in enumerate(reversed(steps)):
-        mine, partner = partner_of(axis, bit)
-        copy = pltpu.make_async_remote_copy(
-            src_ref=table_ref.at[pl.ds(lo, size)],
-            dst_ref=table_ref.at[pl.ds(lo, size)],
-            send_sem=send.at[len(steps) + t],
-            recv_sem=recv.at[len(steps) + t],
-            device_id=partner,
-            device_id_type=MESH,
-        )
-        copy.start()
-        copy.wait()
-        lo = lo - mine * size
-        size = size * 2
-
-
-def centroid_table(sums, counts, nr, nc):
-    chunks = nr * nc
-    own = counts.shape[0] // chunks
-    counts = counts.reshape(chunks, own, K)
-    pad = -own % 8
-    part = jnp.concatenate(
-        [sums.reshape(chunks, own * SUB, K), jnp.pad(counts, ((0, 0), (0, pad), (0, 0)))], axis=1
-    )
-    steps = [("cols", b) for b in range(bits(nc))] + [("rows", b) for b in range(bits(nr))]
-    vmem = pl.BlockSpec(memory_space=pltpu.VMEM)
-    table = pl.pallas_call(
-        functools.partial(table_kernel, steps, nc),
-        in_specs=[vmem],
-        out_specs=vmem,
-        out_shape=jax.ShapeDtypeStruct((chunks, own * SUB, K), F32),
-        scratch_shapes=[
-            pltpu.VMEM(part.shape, F32),
-            pltpu.VMEM(part.shape, F32),
-            pltpu.SemaphoreType.DMA((2 * len(steps),)),
-            pltpu.SemaphoreType.DMA((2 * len(steps),)),
-        ],
-        compiler_params=pltpu.CompilerParams(
-            collective_id=0, has_side_effects=True, vmem_limit_bytes=VMEM_BYTES
-        ),
-        name="centroid_table",
-    )(part)
-    return table.reshape(sums.shape)
-
-
 def remote(src, dst, send, recv, index, partner):
     return pltpu.make_async_remote_copy(
         src_ref=src,
@@ -251,6 +198,91 @@
         device_id=partner,
         device_id_type=MESH,
     )
+
+
+def table_kernel(parts, copies, part_ref, table_ref, acc, landing, send, recv):
+    chunks = part_ref.shape[0]
+    sums = table_ref.shape[1]
+    steps = parts[0][1]
+    enter(steps)
+    lows = [0] * len(parts)
+    half = chunks // 2
+    offset = 0
+    sem = 0
+    for t in range(len(steps)):
+        source = part_ref if t == 0 else acc
+        pending = []
+        for i, (lanes, order) in enumerate(parts):
+            mine, partner = partner_of(*order[t])
+            away = lows[i] + (1 - mine) * half
+            keep = lows[i] + mine * half
+            copy = remote(
+                source.at[pl.ds(away, half), :, lanes],
+                landing.at[pl.ds(offset, half), :, lanes],
+                send,
+                recv,
+                sem,
+                partner,
+            )
+            copy.start()
+            pending.append((copy, keep))
+            sem += 1
+        for i, (lanes, order) in enumerate(parts):
+            copy, keep = pending[i]
+            copy.wait()
+            acc[pl.ds(keep, half), :, lanes] = (
+                source[pl.ds(keep, half), :, lanes] + landing[pl.ds(offset, half), :, lanes]
+            )
+            lows[i] = keep
+        offset += half
+        half = half // 2
+    for i, (lanes, order) in enumerate(parts):
+        for j in range(sums // SUB):
+            count = acc[lows[i], sums + j : sums + j + 1, lanes] * (1.0 / copies)
+            rows = slice(j * SUB, (j + 1) * SUB)
+            table_ref[lows[i], rows, lanes] = acc[lows[i], rows, lanes] / count
+    size = 1
+    for t in reversed(range(len(steps))):
+        pending = []
+        for i, (lanes, order) in enumerate(parts):
+            mine, partner = partner_of(*order[t])
+            ref = table_ref.at[pl.ds(lows[i], size), :, lanes]
+            pending.append(remote(ref, ref, send, recv, sem, partner))
+            pending[-1].start()
+            lows[i] = lows[i] - mine * size
+            sem += 1
+        for copy in pending:
+            copy.wait()
+        size = size * 2
+
+
+def centroid_table(part, own, nr, nc):
+    chunks = nr * nc
+    cols = [("cols", b) for b in range(bits(nc))]
+    rows = [("rows", b) for b in range(bits(nr))]
+    parts = [
+        (slice(0, K // 2), cols + rows),
+        (slice(K // 2, K), cols[:1] + rows[:1] + cols[1:] + rows[1:]),
+    ]
+    sems = 4 * (len(cols) + len(rows))
+    vmem = pl.BlockSpec(memory_space=pltpu.VMEM)
+    table = pl.pallas_call(
+        functools.partial(table_kernel, parts, nc),
+        in_specs=[vmem],
+        out_specs=vmem,
+        out_shape=jax.ShapeDtypeStruct((chunks, own * SUB, K), F32),
+        scratch_shapes=[
+            pltpu.VMEM(part.shape, F32),
+            pltpu.VMEM(part.shape, F32),
+            pltpu.SemaphoreType.DMA((sems,)),
+            pltpu.SemaphoreType.DMA((sems,)),
+        ],
+        compiler_params=pltpu.CompilerParams(
+            collective_id=0, has_side_effects=True, vmem_limit_bytes=VMEM_BYTES
+        ),
+        name="centroid_table",
+    )(part)
+    return table.reshape(chunks * own * SUB, K)
 
 
 def gather_cross_kernel(parts, steps, part_ref, full_ref, acc, landing, send, recv):
@@ -426,21 +458,23 @@
         copy = remote(ref, ref, send, recv, sem, partner)
         sem += 1
         copy.start()
+        if t == len(row_steps) - 1:
+            first.wait()
+            held = held + after
+            for (_, neighbour), (_, place_bit) in list(zip(partners, col_steps))[1:]:
+                copies = []
+                for block in held:
+                    ref = all_codes.at[block]
+                    copies.append(remote(ref, ref, send, recv, sem, neighbour))
+                    sem += 1
+                    copies[-1].start()
+                for other in copies:
+                    other.wait()
+                side = partner_of("cols", place_bit)[0]
+                held = held + [block + (1 - 2 * side) * (1 << place_bit) for block in held]
         copy.wait()
         lo = lo - mine * size
         size = size * 2
-    first.wait()
-    held = held + after
-    for (mine, partner), (axis, bit) in list(zip(partners, col_steps))[1:]:
-        copies = []
-        for block in held:
-            ref = all_codes.at[block]
-            copies.append(remote(ref, ref, send, recv, sem, partner))
-            sem += 1
-            copies[-1].start()
-        for copy in copies:
-            copy.wait()
-        held = held + [block + (1 - 2 * mine) * (1 << bit) for block in held]
     for stays, copy in sends:
 
         @pl.when(jnp.logical_not(stays))
@@ -475,7 +509,7 @@
     return rows.reshape(nr * height // nc, nc * width), all_codes.reshape(-1, codes.shape[1])
 
 
-def iterate_kernel(cross_ref, out_ref, hi, lo, own, landing, total, send, recv):
+def iterate_kernel(cross_ref, out_ref, hi, lo, own, near_gram, landing, total, send, recv):
     size = cross_ref.shape[0]
     half = size // 2
     tile = half // 2
@@ -500,43 +534,56 @@
         lo[rows, :] = l
 
     nn = (((1,), (0,)), ((), ()))
+    own_half = pl.ds(pl.multiple_of(mine * half, half), half)
+    other_half = pl.ds(pl.multiple_of((1 - mine) * half, half), half)
+
+    def sent(slot, t):
+        rows = pl.ds(t * tile, tile)
+        return pltpu.make_async_remote_copy(
+            src_ref=own.at[rows, :],
+            dst_ref=landing.at[slot, rows, :],
+            send_sem=send.at[slot, t],
+            recv_sem=recv.at[slot, t],
+            device_id=partner,
+            device_id_type=MESH,
+        )
+
+    def take(slot):
+        for t in range(2):
+            rows = pl.ds(pl.multiple_of((1 - mine) * half + t * tile, tile), tile)
+            sent(slot, t).wait()
+            h, l = split(landing[slot, t * tile : (t + 1) * tile, :])
+            hi[rows, :] = h
+            lo[rows, :] = l
 
     @pl.loop(0, NS_ITERS - 1)
     def _(step):
         slot = step % 2
-
-        def sent(t):
-            rows = pl.ds(t * tile, tile)
-            return pltpu.make_async_remote_copy(
-                src_ref=own.at[rows, :],
-                dst_ref=landing.at[slot, rows, :],
-                send_sem=send.at[slot, t],
-                recv_sem=recv.at[slot, t],
-                device_id=partner,
-                device_id_type=MESH,
-            )
+        near = (hi[own_half, :], lo[own_half, :])
+        near_gram[...] = dot3(near, near, NT)
+
+        @pl.when(step > 0)
+        def _():
+            take((step + 1) % 2)
 
         for t in range(2):
             rows = pl.ds(pl.multiple_of(mine * half + t * tile, tile), tile)
+            here = slice(t * tile, (t + 1) * tile)
             xh, xl = hi[rows, :], lo[rows, :]
-            gram = dot3((xh, xl), (hi[...], lo[...]), NT)
+            far = (hi[other_half, :], lo[other_half, :])
+            far_gram = dot3((xh, xl), far, NT)
             x = xh.astype(F32) + xl.astype(F32)
-            own[t * tile : (t + 1) * tile, :] = 1.5 * x - 0.5 * dot3(
-                split(gram), (hi[...], lo[...]), nn
-            )
-            sent(t).start()
+            cubic = dot3(split(near_gram[here, :]), (hi[own_half, :], lo[own_half, :]), nn)
+            cubic = cubic + dot3(split(far_gram), far, nn)
+            own[here, :] = 1.5 * x - 0.5 * cubic
+            sent(slot, t).start()
         for t in range(2):
             rows = pl.ds(pl.multiple_of(mine * half + t * tile, tile), tile)
             h, l = split(own[t * tile : (t + 1) * tile, :])
             hi[rows, :] = h
             lo[rows, :] = l
-        for t in range(2):
-            rows = pl.ds(pl.multiple_of((1 - mine) * half + t * tile, tile), tile)
-            sent(t).wait()
-            h, l = split(landing[slot, t * tile : (t + 1) * tile, :])
-            hi[rows, :] = h
-            lo[rows, :] = l
-
+
+    take((NS_ITERS - 2) % 2)
     height, width = out_ref.shape
     r, c = lax.axis_index("rows"), lax.axis_index("cols")
     rows = pl.ds(pl.multiple_of(r * height, height), height)
@@ -559,6 +606,7 @@
             pltpu.VMEM((size, size), BF16),
             pltpu.VMEM((size, size), BF16),
             pltpu.VMEM((size // 2, size), F32),
+            pltpu.VMEM((size // 2, size // 2), F32),
             pltpu.VMEM((2, size // 2, size), F32),
             pltpu.VMEM((8, size), F32),
             pltpu.SemaphoreType.DMA((2, 2)),
@@ -571,17 +619,11 @@
     )(cross)
 
 
-def matmul_high(left, right, dims):
-    return lax.dot_general(
-        left, right, dims, precision=lax.Precision.HIGH, preferred_element_type=F32
-    )
-
-
 def shards(nr, nc, points, codes, rotation):
     own_rows, all_codes = gather_inputs(rotation, codes, nr, nc)
-    rotated = matmul_high(own_rows, points, (((0,), (1,)), ((), ())))
-    sums, counts = code_sums(all_codes, rotated)
-    table = centroid_table(sums, counts, nr, nc)
+    chunks = nr * nc
+    part = code_sums(all_codes, own_rows, points, chunks)
+    table = centroid_table(part, all_codes.shape[0] // chunks, nr, nc)
     c = lax.axis_index("cols")
     local = codes.shape[0]
     own = lax.dynamic_slice_in_dim(table, c * local * SUB, local * SUB, 0)

time: 272 us -> 246 us (0.904)
  matrix products: 14.5 us -> 0 us
  Pallas kernels: 249 us -> 241 us
    dot_general x1 -> x0, matrix products: 14.5 us -> none  [matmul_high(): lax.dot_general(left, right, dims, precision=lax.Precision.HIGH, preferre...]
    pallas_call x1, Pallas kernels: 46.3 us -> 39.9 us  [centroid_table(): pl.pallas_call(functools.partial(table_kernel, parts, nc), in_specs=[vmem...]
    pallas_call x1, Pallas kernels: 24.6 us -> 30.5 us  [code_sums(): pl.pallas_call(code_sums_kernel, grid=(subspaces // block,), in_specs=[pl...]
    pallas_call x1, Pallas kernels: 54.5 us -> 49 us  [new_rotation(): pl.pallas_call(iterate_kernel, in_specs=[vmem], out_specs=vmem, out_shape...]
where the time goes in v1:
time: 246 us
  Pallas kernels  241 us (98%)
  local copies, waits for them, and re-layouts  3.99 us (2%)
    pallas_call x1, Pallas kernels, gather_cross(): pl.pallas_call(functools.partial(gather_cross_kernel, parts, rows + cols)...  58.6 us
    pallas_call x1, Pallas kernels, new_rotation(): pl.pallas_call(iterate_kernel, in_specs=[vmem], out_specs=vmem, out_shape...  49 us
    pallas_call x1, Pallas kernels, gather_inputs(): pl.pallas_call(functools.partial(gather_inputs_kernel, row_steps, col_ste...  39.9 us
    pallas_call x1, Pallas kernels, centroid_table(): pl.pallas_call(functools.partial(table_kernel, parts, nc), in_specs=[vmem...  39.9 us
    pallas_call x1, Pallas kernels, code_sums(): pl.pallas_call(code_sums_kernel, grid=(subspaces // block,), in_specs=[pl...  30.5 us
    pallas_call x1, Pallas kernels, cross_terms(): pl.pallas_call(cross_kernel, grid=(subspaces // block,), in_specs=[pl.Blo...  23.5 us

profile of v1, /device:TPU:0, one launch (start us, length us, event | category | flops | bytes accessed | tf_op | source)
XLA Modules:
  0.0 246.0 jit_solution(14081191990962146350)
XLA Ops:
  0.6 39.9 %gather_inputs.1 = (f32[8,32,1024]{2,1,0:T(8,128)}, s32[4,32,3072]{2,1,0:T(8,128)}) custom-call(f32[128,256]{1,0:T(8,128)} %rot_ref.1, s32[32,3072]{1,0:T(8,128)} %codes_ref.1), custom_call_target="tpu_custom_call" | custom-call | tf_op jit(solution)/shard_map/gather_inputs/pallas_call | solution.py:491
  40.5 30.5 %code_sums.1.part_ref = f32[32,40,256]{2,1,0:T(8,128)} custom-call(s32[128,3072]{1,0:T(8,128)} %bitcast.11, f32[256,1024]{1,0:T(8,128)} %bitcast.17, f32[3072,256]{1,0:T(8,128)} %points_ref.3), custom_call_target="tpu_custom_call" | custom-call | tf_op jit(solution)/shard_map/code_sums/pallas_call | solution.py:106
  71.0 39.9 %centroid_table.1 = f32[32,32,256]{2,1,0:T(8,128)} custom-call(f32[32,40,256]{2,1,0:T(8,128)} %code_sums.1.part_ref), custom_call_target="tpu_custom_call" | custom-call | tf_op jit(solution)/shard_map/centroid_table/pallas_call | solution.py:269
  110.9 23.5 %cross_terms.1 = f32[256,1024]{1,0:T(8,128)} custom-call(s32[128,3072]{1,0:T(8,128)} %bitcast.12, f32[1024,256]{1,0:T(8,128)} %bitcast.13, f32[3072,256]{1,0:T(8,128)} %points_ref.3), custom_call_target="tpu_custom_call" | custom-call | tf_op jit(solution)/shard_map/cross_terms/pallas_call | solution.py:155
  134.4 1.0 dynamic-slice_bitcast_fusion
  135.3 0.4 copy.5
  135.8 1.0 copy.6
  136.8 58.6 %gather_cross.1 = f32[4,8,32,1024]{3,2,1,0:T(8,128)} custom-call(f32[8,32,1024]{2,1,0:T(8,128)} %bitcast.16), custom_call_target="tpu_custom_call" | custom-call | tf_op jit(solution)/shard_map/gather_cross/pallas_call | solution.py:363
  195.4 49.0 %new_rotation.1 = f32[128,256]{1,0:T(8,128)} custom-call(f32[1024,1024]{1,0:T(8,128)} %bitcast.10), custom_call_target="tpu_custom_call" | custom-call | tf_op jit(solution)/shard_map/new_rotation/pallas_call | solution.py:600
  244.4 1.6 copy.8

commit v2 on v1

--- a/solution.py
+++ b/solution.py
@@ -379,11 +379,12 @@
     return full.reshape(nc * d, width)
 
 
-def reversed_bits(index, count):
-    out = 0
-    for b in range(count):
-        out = out + ((index // (1 << b)) % 2) * (1 << (count - 1 - b))
-    return out
+def to_place_of(index, order):
+    return sum(((index // (1 << b)) % 2) * (1 << k) for k, b in enumerate(order))
+
+
+def from_place(place, order):
+    return sum(((place // (1 << k)) % 2) * (1 << b) for k, b in enumerate(order))
 
 
 def gather_inputs_kernel(row_steps, col_steps, rot_ref, codes_ref, rows_ref, all_codes, send, recv, own_sem):
@@ -391,15 +392,19 @@
     nc = all_codes.shape[0]
     width = rot_ref.shape[1]
     r, c = lax.axis_index("rows"), lax.axis_index("cols")
-    place = reversed_bits(r, len(row_steps))
-    source = (c * nr + place) // nc
-    is_own = source == r
+    row_bits = [b for _, b in row_steps]
+    orders = [row_bits[::-1], row_bits[:1] + row_bits[:0:-1]]
+    places = [to_place_of(r, order) for order in orders]
+    sources = [(c * nr + place) // nc for place in places]
+    band_of = [j * 2 // nc for j in range(nc)]
+    first_band = c < nc // 2
+    is_own = jnp.where(first_band, sources[0], sources[1]) == r
     barrier = pltpu.get_barrier_semaphore()
     for j in range(nc):
 
         @pl.when(jnp.logical_not(is_own & (c == j)))
         def _():
-            pl.semaphore_signal(barrier, inc=1, device_id=(source, j), device_id_type=MESH)
+            pl.semaphore_signal(barrier, inc=1, device_id=(sources[band_of[j]], j), device_id_type=MESH)
 
     for axis, bit in row_steps + col_steps:
         pl.semaphore_signal(barrier, inc=1, device_id=partner_of(axis, bit)[1], device_id_type=MESH)
@@ -416,7 +421,9 @@
     for i in range(nc):
         g = r * nc + i
         to_c, to_place = g // nr, g % nr
-        to_r = reversed_bits(to_place, len(row_steps))
+        to_r = jnp.where(
+            first_band, from_place(to_place, orders[0]), from_place(to_place, orders[1])
+        )
         src = rot_ref.at[pl.ds(i * piece, piece), :]
         dst = rows_ref.at[to_place, :, lanes]
         stays = (to_c == c) & (to_r == r)
@@ -445,19 +452,24 @@
 
         @pl.when(jnp.logical_not(is_own & (c == j)))
         def _():
-            ref = rows_ref.at[place, :, pl.ds(j * width, width)]
+            ref = rows_ref.at[places[band_of[j]], :, pl.ds(j * width, width)]
             remote(ref, ref, send, recv, j, partners[0][1]).wait_recv()
 
-    lo, size = place, 1
+    lows, size = list(places), 1
+    middle = rows_ref.shape[2] // 2
+    bands = [slice(0, middle), slice(middle, 2 * middle)]
     held = [c]
     mine, partner = partners[0]
     after = [c + (1 - 2 * mine) * (1 << col_steps[0][1])]
-    for t, (axis, bit) in enumerate(reversed(row_steps)):
-        mine, partner = partner_of(axis, bit)
-        ref = rows_ref.at[pl.ds(lo, size)]
-        copy = remote(ref, ref, send, recv, sem, partner)
-        sem += 1
-        copy.start()
+    for t in range(len(row_steps)):
+        moving = []
+        for i in range(2):
+            mine, partner = partner_of("rows", orders[i][t])
+            ref = rows_ref.at[pl.ds(lows[i], size), :, bands[i]]
+            moving.append(remote(ref, ref, send, recv, sem, partner))
+            sem += 1
+            moving[-1].start()
+            lows[i] = lows[i] - mine * size
         if t == len(row_steps) - 1:
             first.wait()
             held = held + after
@@ -472,8 +484,8 @@
                     other.wait()
                 side = partner_of("cols", place_bit)[0]
                 held = held + [block + (1 - 2 * side) * (1 << place_bit) for block in held]
-        copy.wait()
-        lo = lo - mine * size
+        for copy in moving:
+            copy.wait()
         size = size * 2
     for stays, copy in sends:
 
@@ -487,7 +499,7 @@
     row_steps = [("rows", b) for b in range(bits(nr))]
     col_steps = [("cols", b) for b in reversed(range(bits(nc)))]
     vmem = pl.BlockSpec(memory_space=pltpu.VMEM)
-    sems = 3 * nc + len(row_steps)
+    sems = 3 * nc + 2 * len(row_steps)
     rows, all_codes = pl.pallas_call(
         functools.partial(gather_inputs_kernel, row_steps, col_steps),
         in_specs=[vmem, vmem],

time: 246 us -> 241 us (0.980)
  Pallas kernels: 241 us -> 236 us
    pallas_call x1, Pallas kernels: 39.9 us -> 33.3 us  [gather_inputs(): pl.pallas_call(functools.partial(gather_inputs_kernel, row_steps, col_ste...]
    pallas_call x1, Pallas kernels: 39.9 us -> 43.4 us  [centroid_table(): pl.pallas_call(functools.partial(table_kernel, parts, nc), in_specs=[vmem...]
where the time goes in v2:
time: 241 us
  Pallas kernels  236 us (98%)
  local copies, waits for them, and re-layouts  3.99 us (2%)
    pallas_call x1, Pallas kernels, gather_cross(): pl.pallas_call(functools.partial(gather_cross_kernel, parts, rows + cols)...  56.7 us
    pallas_call x1, Pallas kernels, new_rotation(): pl.pallas_call(iterate_kernel, in_specs=[vmem], out_specs=vmem, out_shape...  49 us
    pallas_call x1, Pallas kernels, centroid_table(): pl.pallas_call(functools.partial(table_kernel, parts, nc), in_specs=[vmem...  43.4 us
    pallas_call x1, Pallas kernels, gather_inputs(): pl.pallas_call(functools.partial(gather_inputs_kernel, row_steps, col_ste...  33.3 us
    pallas_call x1, Pallas kernels, code_sums(): pl.pallas_call(code_sums_kernel, grid=(subspaces // block,), in_specs=[pl...  30.5 us
    pallas_call x1, Pallas kernels, cross_terms(): pl.pallas_call(cross_kernel, grid=(subspaces // block,), in_specs=[pl.Blo...  23.5 us

profile of v2, /device:TPU:0, one launch (start us, length us, event | category | flops | bytes accessed | tf_op | source)
XLA Modules:
  0.0 241.0 jit_solution(15500484041515137149)
XLA Ops:
  0.6 33.3 %gather_inputs.1 = (f32[8,32,1024]{2,1,0:T(8,128)}, s32[4,32,3072]{2,1,0:T(8,128)}) custom-call(f32[128,256]{1,0:T(8,128)} %rot_ref.1, s32[32,3072]{1,0:T(8,128)} %codes_ref.1), custom_call_target="tpu_custom_call" | custom-call | tf_op jit(solution)/shard_map/gather_inputs/pallas_call | solution.py:503
  33.9 30.5 %code_sums.1.part_ref = f32[32,40,256]{2,1,0:T(8,128)} custom-call(s32[128,3072]{1,0:T(8,128)} %bitcast.11, f32[256,1024]{1,0:T(8,128)} %bitcast.17, f32[3072,256]{1,0:T(8,128)} %points_ref.3), custom_call_target="tpu_custom_call" | custom-call | tf_op jit(solution)/shard_map/code_sums/pallas_call | solution.py:106
  64.4 43.4 %centroid_table.1 = f32[32,32,256]{2,1,0:T(8,128)} custom-call(f32[32,40,256]{2,1,0:T(8,128)} %code_sums.1.part_ref), custom_call_target="tpu_custom_call" | custom-call | tf_op jit(solution)/shard_map/centroid_table/pallas_call | solution.py:269
  107.8 23.5 %cross_terms.1 = f32[256,1024]{1,0:T(8,128)} custom-call(s32[128,3072]{1,0:T(8,128)} %bitcast.12, f32[1024,256]{1,0:T(8,128)} %bitcast.13, f32[3072,256]{1,0:T(8,128)} %points_ref.3), custom_call_target="tpu_custom_call" | custom-call | tf_op jit(solution)/shard_map/cross_terms/pallas_call | solution.py:155
  131.3 1.0 dynamic-slice_bitcast_fusion
  132.3 0.4 copy.5
  132.7 1.0 copy.6
  133.7 56.7 %gather_cross.1 = f32[4,8,32,1024]{3,2,1,0:T(8,128)} custom-call(f32[8,32,1024]{2,1,0:T(8,128)} %bitcast.16), custom_call_target="tpu_custom_call" | custom-call | tf_op jit(solution)/shard_map/gather_cross/pallas_call | solution.py:363
  190.4 49.0 %new_rotation.1 = f32[128,256]{1,0:T(8,128)} custom-call(f32[1024,1024]{1,0:T(8,128)} %bitcast.10), custom_call_target="tpu_custom_call" | custom-call | tf_op jit(solution)/shard_map/new_rotation/pallas_call | solution.py:612
  239.4 1.6 copy.8
